TPU v7x, 32 devices: a whole 2x2x4 slice. The times are simulated.
32 devices in a mesh: dp: 16 (over z, y, core), mp: 2 (over x).
Axes of the slice: x: 2, y: 2, z: 4, core: 2. Of those that a mesh axis runs over, the one named last changes fastest.
Arguments:
- residual: bfloat16 [4096, 4608], P('dp', 'mp'), may hold values from -6 to 6
- out_grad: bfloat16 [4096, 4608], P('dp', 'mp'), may hold values from -6 to 6
- ffn_weights: bfloat16 [3, 64, 4608], P(None, 'mp'), may hold values from -0.09375 to 0.09375
- norm_gain: float32 [4608], replicated, may hold values from 0.1 to 1.9
- exponents: int32 [3], replicated, may hold values from 3 to 6, as said below
- sign_bits: int32 [4608], replicated, may hold values from 0 to 1
Outputs:
- resid_grad: bfloat16 [4096, 4608], P('dp', 'mp')
- weight_grads: bfloat16 [3, 64, 4608], P(None, 'mp')
Inputs may be any that keep to these rules, and one draw needn't show every extreme that they name: `exponents`: one exponent for each of the gate, up and down gradients; every draw holds both 3 and 6. `sign_bits`: one bit per feature.
All inputs are finite; a program needn't handle non-finite values.
Results may differ from a plain program's by a relative error of at most 0.01.
Values may be sent and summed in bfloat16 or wider, within the bound.
A program may use at most 64 MiB of HBM per device.

v0:
```python
import math

import jax
import jax.numpy as jnp
from jax import lax
from jax.sharding import PartitionSpec as P


def hadamard():
    indices = jnp.arange(128, dtype=jnp.int32)
    anded = jnp.bitwise_and(indices[:, None], indices[None, :])
    parity = jnp.zeros((128, 128), jnp.int32)
    for offset in range(7):
        parity = parity + jnp.bitwise_and(jnp.right_shift(anded, offset), 1)
    return (1 - 2 * (parity % 2)).astype(jnp.float32) / math.sqrt(128.0)


def gelu_parts(values):
    tanh_input = 0.7978845608 * (values + 0.044715 * values * values * values)
    tanhed = jnp.tanh(tanh_input)
    forward = 0.5 * values * (1.0 + tanhed)
    gelu_slope = 0.5 * (1.0 + tanhed) + 0.5 * values * (1.0 - tanhed * tanhed) * 0.7978845608 * (
        1.0 + 3.0 * 0.044715 * values * values
    )
    return (forward, gelu_slope)


def restore(summed, factors, sign_table, hadamard_table):
    block_count = sign_table.shape[0]
    widened = lax.optimization_barrier(summed).astype(jnp.float32).reshape(3, -1, block_count, 128)
    scaled = widened * factors[:, None, None, None]
    restored = (
        jnp.einsum("kubj,jc->kubc", scaled, hadamard_table, precision=lax.Precision.HIGHEST)
        * sign_table
    )
    return restored.astype(jnp.bfloat16).reshape(3, -1, block_count * 128)


def per_device(residual, out_grad, ffn_weights, norm_gain, exponents, sign_bits):
    full_rows, grads_in = (
        lax.all_gather(residual, "mp", axis=1, tiled=True),
        lax.all_gather(out_grad, "mp", axis=1, tiled=True),
    )
    feature_count = full_rows.shape[1]
    col_count = residual.shape[1]
    col_start = lax.axis_index("mp") * col_count
    bucket_rows = ffn_weights.shape[1]
    rows_wide = full_rows.astype(jnp.float32)
    inverse = lax.rsqrt(jnp.mean(rows_wide * rows_wide, axis=1, keepdims=True) + 1e-06)
    unit_rows = rows_wide * inverse
    normed = (unit_rows * norm_gain).astype(jnp.bfloat16)
    pair_weights = ffn_weights[:2]
    gate_up = jnp.einsum("td,khd->tkh", normed, pair_weights, preferred_element_type=jnp.float32)
    gate_pre = gate_up[:, 0]
    up_proj = gate_up[:, 1]
    activated, gelu_slope = gelu_parts(gate_pre)
    hidden = (activated * up_proj).astype(jnp.bfloat16)
    hidden_grad = lax.dot_general(
        grads_in, ffn_weights[2], (((1,), (1,)), ((), ())), preferred_element_type=jnp.float32
    )
    gate_grad = (hidden_grad * up_proj * gelu_slope).astype(jnp.bfloat16)
    up_grad = (hidden_grad * activated).astype(jnp.bfloat16)
    pair_grad = jnp.stack([gate_grad, up_grad], axis=1)
    partial_value = jnp.einsum(
        "tkh,khd->td", pair_grad, pair_weights, preferred_element_type=jnp.float32
    )
    own_unit = lax.dynamic_slice_in_dim(unit_rows, col_start, col_count, 1)
    normed_grad = lax.psum(partial_value.astype(jnp.bfloat16), "mp").astype(jnp.float32)
    feature_grad = normed_grad * norm_gain
    row_mean = jnp.sum(feature_grad * unit_rows, axis=1, keepdims=True) / feature_count
    own_grad = lax.dynamic_slice_in_dim(feature_grad, col_start, col_count, 1)
    resid_grad = (out_grad.astype(jnp.float32) + inverse * (own_grad - own_unit * row_mean)).astype(
        jnp.bfloat16
    )
    pair_wgrad = jnp.einsum("tkh,td->khd", pair_grad, normed, preferred_element_type=jnp.float32)
    down_wgrad = lax.dot_general(
        hidden, grads_in, (((0,), (0,)), ((), ())), preferred_element_type=jnp.float32
    )
    stacked = jnp.concatenate([pair_wgrad, down_wgrad[None]], axis=0)
    block_count = feature_count // 128
    sign_table = (2 * sign_bits - 1).astype(jnp.float32).reshape(block_count, 128)
    hadamard_table = hadamard()
    shaped = stacked.reshape(3, bucket_rows, block_count, 128) * sign_table
    rotated = jnp.einsum("kubj,jc->kubc", shaped, hadamard_table, precision=lax.Precision.HIGHEST)
    scales = jnp.exp2(exponents.astype(jnp.float32))
    quantized = jnp.clip(rotated * scales[:, None, None, None], -127.0, 127.0).astype(jnp.bfloat16)
    flat_terms = lax.optimization_barrier(quantized).astype(jnp.float32).reshape(-1, 128)
    factors = jnp.exp2(-exponents.astype(jnp.float32)) / float(lax.axis_size("dp"))
    own_share = lax.psum_scatter(flat_terms, "dp", scatter_dimension=0, tiled=True).astype(
        jnp.bfloat16
    )
    gathered = lax.all_gather(own_share, "dp", axis=0, tiled=True)
    weight_grads = restore(gathered, factors, sign_table, hadamard_table)
    return (resid_grad, weight_grads)


def solution(mesh):
    placed = (P("dp", "mp"), P("dp", "mp"), P(None, "mp", None), P(), P(), P())
    return jax.shard_map(
        per_device,
        mesh=mesh,
        in_specs=placed,
        out_specs=(P("dp", "mp"), P(None, "mp", None)),
        check_vma=False,
    )
```

profile of v0, /device:TPU:1, one launch (start us, length us, event | category | flops | bytes accessed | tf_op | source)
XLA Modules:
  0.0 256.3 jit_solution(725584316986459335)
XLA Ops:
  7.2 0.0 copy-start.9
  7.2 0.0 copy-start.3
  7.2 0.0 all-gather.3.cloned.1.call-start
  7.2 0.7 all-gather.3.cloned.1.call-update
  7.9 0.0 all-gather.5.cloned.1.call-start
  8.0 0.7 all-gather.5.cloned.1.call-update
  8.7 0.0 all-reduce.3.cloned.1.call-start
  8.7 39.0 %all-gather.3.cloned.1.call-done = bf16[256,4608]{1,0:T(8,128)(2,1)} async-done(((bf16[256,2304]{1,0:T(8,128)(2,1)}), bf16[256,4608]{1,0:T(8,128)(2,1)}) %all-gather.3.cloned.1.call-update) | async-done | bytes 2359312 | tf_op jit(solution)/shard_map/all_gather | solution.py:41
  47.7 0.0 copy-start
  47.7 2.4 fusion.1
  50.1 0.0 copy-start.11
  50.1 0.5 copy-done.11
  50.7 0.0 copy-done.9
  50.7 0.0 copy-done.3
  50.7 0.0 copy-done
  50.7 0.9 fusion.13
  51.6 0.0 copy-start.6
  51.6 33.8 %all-gather.5.cloned.1.call-done = bf16[256,4608]{1,0:T(8,128)(2,1)} async-done(((bf16[256,2304]{1,0:T(8,128)(2,1)}), bf16[256,4608]{1,0:T(8,128)(2,1)}) %all-gather.5.cloned.1.call-update) | async-done | bytes 2359312 | tf_op jit(solution)/shard_map/all_gather | solution.py:42
  85.4 2.4 fusion.64
  87.8 0.0 copy-start.8
  87.9 0.0 copy-start.14
  87.9 0.0 copy-start.10
  87.9 2.2 fusion
  90.1 0.0 copy-done.6
  90.1 0.0 all-reduce.3.cloned.1.call-update
  90.1 0.0 copy-done.8
  90.1 0.0 reduce-scatter.4.cloned.1.call-start
  90.2 0.0 copy-done.14
  90.2 0.6 exponential_multiply_fusion
  90.8 0.0 copy-done.10
  90.8 0.6 convert_bitcast_fusion
  91.4 1.6 fusion.15
  92.9 1.3 concatenate.6
  94.2 0.0 copy-start.7
  94.2 4.4 %copy.12 = bf16[4608,256]{1,0:T(8,128)(2,1)} copy(bf16[4608,256]{0,1:T(8,128)(2,1)} %bitcast.58) | data formatting | bytes 4718592 | tf_op jit(solution)/shard_map/dot_general | solution.py:76
  98.6 0.0 copy-start.2
  98.6 0.0 copy-start.4
  98.6 0.0 copy-start.15
  98.6 0.0 copy-done.7
  98.6 2.6 convolution_bitcast_fusion.1
  101.2 0.4 copy.13
  101.5 0.0 copy-done.2
  101.5 0.0 copy-done.4
  101.6 0.0 copy-done.15
  101.6 1.8 clamp_convert_fusion
  103.3 0.0 copy-start.12
  103.3 1.4 reshape.51
  104.8 0.0 reduce-scatter.4.cloned.1.call-update
  104.8 0.0 copy-start.1
  104.8 54.1 %all-reduce.3.cloned.1.call-done = bf16[256,4608]{1,0:T(8,128)(2,1)} async-done(((bf16[256,4608]{1,0:T(8,128)(2,1)}), bf16[256,4608]{1,0:T(8,128)(2,1)}) %all-reduce.3.cloned.1.call-update) | async-done | bytes 2359312 | tf_op jit(solution)/shard_map/psum | solution.py:68
  158.9 0.0 copy-done.12
  158.9 2.7 %multiply_reduce_fusion = (f32[256]{0:T(256)S(1)}, f32[256,4608]{1,0:T(8,128)S(1)}, f32[256,4608]{1,0:T(8,128)S(1)}) fusion(f32[4608]{0:T(1024)} %param.9, bf16[256,4608]{1,0:T(8,128)(2,1)} %all-reduce.3.cloned.1.call-done, f32[256]{0:T(256)S(1)} %copy-done.12, bf16[256,4608]{1,0:T(8,128)(2,1)S(1)} %copy-done), kind=kLoop, calls=%fused_computation.5 | loop fusion | flops 7077632 | bytes 14176256 | tf_op jit(solution)/shard_map/reduce_sum | solution.py:70
  161.6 0.0 copy-done.1
  161.7 1.6 add_convert_fusion
  163.2 0.0 copy-start.5
  163.2 0.0 copy-start.13
  163.2 58.5 %reduce-scatter.4.cloned.1.call-done = f32[216,128]{1,0:T(8,128)} async-done(((f32[3456,128]{1,0:T(8,128)}), f32[216,128]{1,0:T(8,128)}) %reduce-scatter.4.cloned.1.call-update) | async-done | bytes 110608
  221.8 0.9 convert_element_type.67
  222.7 23.8 %all_gather.11 = bf16[3456,128]{1,0:T(8,128)(2,1)S(1)} all-gather(bf16[216,128]{1,0:T(8,128)(2,1)S(1)} %convert_element_type.67), channel_id=1, replica_groups=mesh['dp'=16,'mp'=2] {'dp'}, dimensions={0}, use_global_device_ids=true | all-gather | bytes 940032 | tf_op jit(solution)/shard_map/all_gather | solution.py:92
  246.5 0.1 reshape.53
  246.6 0.0 copy-done.5
  246.6 0.0 copy-done.13
  246.6 1.8 multiply_convert_fusion.1
  248.4 1.4 reshape.49
  (2 shorter events, 0.0 us)
Async XLA Ops:
  7.2 43.5 %copy-start.9 = (f32[4608]{0:T(1024)S(1)}, f32[4608]{0:T(1024)}, u32[]{:S(2)}) copy-start(f32[4608]{0:T(1024)} %param.9) | copy-start | bytes 55300
  7.2 43.5 %copy-start.3 = (bf16[3,32,4608]{2,1,0:T(8,128)(2,1)S(1)}, bf16[3,32,4608]{2,1,0:T(8,128)(2,1)}, u32[]{:S(2)}) copy-start(bf16[3,32,4608]{2,1,0:T(8,128)(2,1)} %param.8) | copy-start | bytes 2654212
  7.2 40.6 %all-gather.3.cloned.1.call-start = ((), (), s32[]{:S(2)}) async-start(), calls=%async_computation.1 | async-start | bytes 3538944 | tf_op jit(solution)/shard_map/all_gather | solution.py:41
  7.9 77.5 %all-gather.5.cloned.1.call-start = ((), (), s32[]{:S(2)}) async-start(), calls=%async_computation.2 | async-start | bytes 3538944 | tf_op jit(solution)/shard_map/all_gather | solution.py:42
  8.7 150.3 %all-reduce.3.cloned.1.call-start = ((), (), s32[]{:S(2)}) async-start(), calls=%async_computation.3 | async-start | bytes 4718592 | tf_op jit(solution)/shard_map/psum | solution.py:68
  47.7 2.9 %copy-start = (bf16[256,4608]{1,0:T(8,128)(2,1)S(1)}, bf16[256,4608]{1,0:T(8,128)(2,1)}, u32[]{:S(2)}) copy-start(bf16[256,4608]{1,0:T(8,128)(2,1)} %all-gather.3.cloned.1.call-done) | copy-start | bytes 7077892
  50.1 0.5 copy-start.11
  51.6 38.5 %copy-start.6 = (f32[256,2,32]{0,2,1:T(8,128)}, f32[256,2,32]{0,2,1:T(8,128)S(1)}, u32[]{:S(2)}) copy-start(f32[256,2,32]{0,2,1:T(8,128)S(1)} %fusion.13) | copy-start | bytes 196612
  87.8 2.3 copy-start.8
  87.9 2.3 copy-start.14
  87.9 2.9 %copy-start.10 = (s32[4608]{0:T(1024)S(1)}, s32[4608]{0:T(1024)}, u32[]{:S(2)}) copy-start(s32[4608]{0:T(1024)} %param.11) | copy-start | bytes 55300
  90.1 131.6 %reduce-scatter.4.cloned.1.call-start = ((), (), s32[]{:S(2)}) async-start(), calls=%async_computation.4 | async-start | bytes 1880064
  94.2 4.4 %copy-start.7 = (f32[256,2,32]{0,2,1:T(8,128)S(1)}, f32[256,2,32]{0,2,1:T(8,128)}, u32[]{:S(2)}) copy-start(f32[256,2,32]{0,2,1:T(8,128)} %copy-done.6) | copy-start | bytes 196612
  98.6 2.9 %copy-start.2 = (f32[2,32,36,128]{3,2,1,0:T(8,128)S(1)}, f32[2,32,36,128]{3,2,1,0:T(8,128)}, u32[]{:S(2)}) copy-start(f32[2,32,36,128]{3,2,1,0:T(8,128)} %concatenate.6) | copy-start | bytes 3538948
  98.6 2.9 %copy-start.4 = (f32[36,128]{1,0:T(8,128)S(1)}, f32[36,128]{1,0:T(8,128)}, u32[]{:S(2)}) copy-start(f32[36,128]{1,0:T(8,128)} %convert_bitcast_fusion) | copy-start | bytes 55300
  98.6 3.0 %copy-start.15 = (f32[3]{0:T(128)S(1)}, f32[3]{0:T(128)}, u32[]{:S(2)}) copy-start(f32[3]{0:T(128)} %get-tuple-element.8) | copy-start | bytes 40
  103.3 55.6 %copy-start.12 = (f32[256]{0:T(256)S(1)}, f32[256]{0:T(256)}, u32[]{:S(2)}) copy-start(f32[256]{0:T(256)} %copy-done.11) | copy-start | bytes 3076
  104.8 56.8 %copy-start.1 = (bf16[256,2304]{1,0:T(8,128)(2,1)S(1)}, bf16[256,2304]{1,0:T(8,128)(2,1)}, u32[]{:S(2)}) copy-start(bf16[256,2304]{1,0:T(8,128)(2,1)} %param.7) | copy-start | bytes 3538948
  163.2 83.4 %copy-start.5 = (f32[36,128]{1,0:T(8,128)S(1)}, f32[36,128]{1,0:T(8,128)}, u32[]{:S(2)}) copy-start(f32[36,128]{1,0:T(8,128)} %convert_bitcast_fusion) | copy-start | bytes 55300
  163.2 83.4 %copy-start.13 = (f32[3]{0:T(128)S(1)}, f32[3]{0:T(128)}, u32[]{:S(2)}) copy-start(f32[3]{0:T(128)} %get-tuple-element.7) | copy-start | bytes 40
Sparse Core Ops, SparseCore 0:
  9.6 38.1 all-gather.2
  49.3 36.0 all-gather.4
  90.3 68.6 all-reduce.2
  163.0 58.6 reduce-scatter.3
where the time goes:
time: 257 us; the launch traced here: 256 us
  waiting for transfers between devices  187 us (73%)
  blocking collectives  23.8 us (9%)
  between operations  14 us (5%)
  matrix products  13.2 us (5%)
  local copies, waits for them, and re-layouts  9.6 us (4%)
  other arithmetic  8.74 us (3%)
    unnamed x5, waiting for transfers between devices  59.9 us
    psum x1, waiting for transfers between devices, per_device(): lax.psum(partial_value.astype(jnp.bfloat16), 'mp').astype(jnp.float32)  54.1 us
    all_gather x1, waiting for transfers between devices, per_device(): lax.all_gather(residual, 'mp', axis=1, tiled=True)  39 us
    all_gather x1, waiting for transfers between devices, per_device(): lax.all_gather(out_grad, 'mp', axis=1, tiled=True)  33.8 us
    all_gather x1, blocking collectives, per_device(): gathered = lax.all_gather(own_share, 'dp', axis=0, tiled=True)  23.8 us
  transfers between devices with their start and end apart: 4, of which 4 were waited for; matrix products, arithmetic and copies ran while one was open for 9% of the time, Pallas kernels for 0%

commit v1 on v0

--- a/solution.py
+++ b/solution.py
@@ -1,9 +1,383 @@
+import functools
 import math
 
 import jax
 import jax.numpy as jnp
 from jax import lax
+from jax.experimental import pallas as pl
+from jax.experimental.pallas import tpu as pltpu
 from jax.sharding import PartitionSpec as P
+
+MESH = pl.DeviceIdType.MESH
+F32 = jnp.float32
+BF16 = jnp.bfloat16
+
+
+def dot_nt(left, right):
+    return lax.dot_general(left, right, (((1,), (1,)), ((), ())), preferred_element_type=F32)
+
+
+def dot_nn(left, right):
+    return lax.dot_general(left, right, (((1,), (0,)), ((), ())), preferred_element_type=F32)
+
+
+def split_dot(dot, left, right, split_left):
+    wide = left if split_left else right
+    high = wide.astype(BF16)
+    low = (wide - high.astype(F32)).astype(BF16)
+    if split_left:
+        return dot(high, right) + dot(low, right)
+    return dot(left, high) + dot(left, low)
+
+
+def signs_256():
+    rows = lax.broadcasted_iota(jnp.int32, (256, 256), 0)
+    cols = lax.broadcasted_iota(jnp.int32, (256, 256), 1)
+    anded = jnp.bitwise_and(jnp.bitwise_and(rows, cols), 127)
+    for shift in (4, 2, 1):
+        anded = jnp.bitwise_xor(anded, jnp.right_shift(anded, shift))
+    value = 1 - 2 * jnp.bitwise_and(anded, 1)
+    same = jnp.right_shift(rows, 7) == jnp.right_shift(cols, 7)
+    return jnp.where(same, value, 0).astype(F32).astype(BF16)
+
+
+def to_column(row):
+    return jnp.broadcast_to(row[0:1], (128, row.shape[1])).T
+
+
+def pair(ref, first):
+    return jnp.concatenate([ref[first], ref[first + 1]], axis=1)
+
+
+def kernel(
+    sizes,
+    res_ref,
+    og_ref,
+    w_ref,
+    gain_ref,
+    exp_ref,
+    sign_ref,
+    rg_ref,
+    out_ref,
+    had,
+    normed,
+    column,
+    wbuf,
+    sq_mine,
+    sq_peer,
+    part,
+    part_out,
+    part_in,
+    terms,
+    core_in,
+    core_sum,
+    y_in,
+    y_sum,
+    z_in,
+    share,
+    slots,
+    local_sem,
+    send_sem,
+    recv_sem,
+):
+    n_dp, blocks, groups, window, starts = sizes
+    cols = blocks * 128
+    per_block = 3 * groups
+    rows_w = 16 * groups
+    half = blocks * per_block // 2
+    quarter = half // 2
+    me = lax.axis_index("dp")
+    side = lax.axis_index("mp")
+    other = 1 - side
+    core = me % 2
+    y = (me // 2) % 2
+    z = me // 4
+    z_near = [z, z + 1 - 2 * (z % 2), (z + 2) % 4, 3 - z]
+    first_block = side * blocks
+    to_x = (me, other)
+    to_core = (me + 1 - 2 * core, side)
+    to_y = (me + 2 - 4 * y, side)
+    to_z = [None] + [(zz * 4 + y * 2 + core, side) for zz in z_near[1:]]
+    count = [0]
+
+    def remote(src, dst, target):
+        index = count[0]
+        count[0] += 1
+        return pltpu.make_async_remote_copy(
+            src_ref=src,
+            dst_ref=dst,
+            send_sem=send_sem.at[index],
+            recv_sem=recv_sem.at[index],
+            device_id=target,
+            device_id_type=MESH,
+        )
+
+    started = []
+
+    def send(copy):
+        copy.start()
+        started.append(copy)
+
+    barrier = pltpu.get_barrier_semaphore()
+    partners = [to_x, to_core, to_y] + to_z[1:]
+    for target in partners:
+        pl.semaphore_signal(barrier, inc=1, device_id=target, device_id_type=MESH)
+
+    own_cols = pl.ds(pl.multiple_of(side * cols, 128), cols)
+    peer_cols = pl.ds(pl.multiple_of(other * cols, 128), cols)
+    own_w = pltpu.make_async_copy(w_ref.at[:, :, own_cols], wbuf.at[side], local_sem)
+    own_w.start()
+    wide = res_ref[...].astype(F32)
+    ones = jnp.ones((8, cols), BF16)
+    sq_mine[...] = split_dot(dot_nt, ones, wide * wide, False)
+    had[...] = signs_256()
+    pl.semaphore_wait(barrier, len(partners))
+
+    sq_copy = remote(sq_mine, sq_peer, to_x)
+    send(sq_copy)
+    core_rows = pl.ds(pl.multiple_of(core * (rows_w // 2), 16), rows_w // 2)
+    w_copies = {}
+    for k in (2, 0, 1):
+        w_copies[k] = remote(
+            w_ref.at[k, core_rows, peer_cols], wbuf.at[side, k, core_rows], to_x
+        )
+        send(w_copies[k])
+
+    own_w.wait()
+    part[side, 2 * rows_w : 3 * rows_w] = dot_nt(wbuf[side, 2], og_ref[...])
+    sq_copy.wait_recv()
+    total_sq = sq_mine[...] + sq_peer[...]
+    inverse = to_column(lax.rsqrt(total_sq / float(2 * cols) + 1e-06))
+    column[0] = inverse
+    for j in range(blocks):
+        at = slice(128 * j, 128 * j + 128)
+        unit = res_ref[:, at].astype(F32) * inverse
+        normed[:, at] = (unit * gain_ref[first_block + j]).astype(BF16)
+    part[side, : 2 * rows_w] = dot_nt(
+        wbuf[side, :2].reshape(2 * rows_w, cols), normed[...]
+    )
+    part_out[side] = part[side].astype(BF16)
+    own_part = remote(part_out.at[side], part_in.at[side], to_x)
+    send(own_part)
+
+    shared = {}
+    for k in (2, 0, 1):
+        w_copies[k].wait_recv()
+        shared[k] = remote(
+            wbuf.at[other, k, core_rows], wbuf.at[other, k, core_rows], to_core
+        )
+        send(shared[k])
+    shared[2].wait_recv()
+    part[other, 2 * rows_w : 3 * rows_w] = dot_nt(wbuf[other, 2], og_ref[...])
+    shared[0].wait_recv()
+    shared[1].wait_recv()
+    part[other, : 2 * rows_w] = dot_nt(
+        wbuf[other, :2].reshape(2 * rows_w, cols), normed[...]
+    )
+    part_out[other] = part[other].astype(BF16)
+    peer_part = remote(part_out.at[other], part_in.at[other], to_x)
+    send(peer_part)
+    own_part.wait_recv()
+    peer_part.wait_recv()
+
+    pair_grads = []
+    hiddens = []
+    row_total = jnp.zeros((1, part.shape[2]), F32)
+    for g in range(2):
+        full = part[g] + part_in[g].astype(F32)
+        gate_pre = full[:rows_w]
+        up_proj = full[rows_w : 2 * rows_w]
+        hidden_grad = full[2 * rows_w :]
+        activated, slope = gelu_parts(gate_pre)
+        hiddens.append((activated * up_proj).astype(BF16))
+        gate_grad = (hidden_grad * up_proj * slope).astype(BF16)
+        up_grad = (hidden_grad * activated).astype(BF16)
+        pair_grads += [gate_grad, up_grad]
+        row_total = row_total + jnp.sum(
+            gate_grad.astype(F32) * gate_pre + up_grad.astype(F32) * up_proj,
+            axis=0,
+            keepdims=True,
+        )
+    pair_grad = jnp.concatenate(pair_grads, axis=0)
+    hidden = jnp.concatenate(hiddens, axis=0)
+
+    scales = [
+        lax.shift_left(jnp.int32(1), exp_ref[k]).astype(F32) * (1.0 / math.sqrt(128.0))
+        for k in range(3)
+    ]
+    order = [(0, 0), (0, 1), (1, 0), (1, 1), (0, 2), (1, 2)]
+    table = had[...]
+    for jj in range(blocks // 2):
+        at = slice(256 * jj, 256 * jj + 256)
+        grads = jnp.concatenate(
+            [dot_nn(pair_grad, normed[:, at]), dot_nn(hidden, og_ref[:, at])], axis=0
+        )
+        bits = pair(sign_ref, first_block + 2 * jj)
+        signed = grads * (2 * bits - 1).astype(F32)
+        rotated = split_dot(dot_nn, signed, table, True)
+        for index, (g, k) in enumerate(order):
+            piece = rotated[index * rows_w : (index + 1) * rows_w] * scales[k]
+            piece = jnp.clip(piece, -127.0, 127.0).astype(BF16)
+            for b in range(2):
+                for i in range(groups):
+                    unit_at = (2 * jj + b) * per_block + k * groups + i
+                    terms[g, unit_at] = piece[16 * i : 16 * i + 16, 128 * b : 128 * b + 128]
+
+    core_copy = remote(terms.at[:, pl.ds(half * (1 - core), half)], core_in, to_core)
+    send(core_copy)
+    column[1] = to_column(row_total / float(2 * cols))
+    core_copy.wait_recv()
+    core_sum[...] = (
+        terms[:, pl.ds(half * core, half)].astype(F32) + core_in[...].astype(F32)
+    ).astype(BF16)
+    y_copy = remote(core_sum.at[:, pl.ds(quarter * (1 - y), quarter)], y_in, to_y)
+    send(y_copy)
+
+    turned = pair_grad.astype(F32).T.astype(BF16)
+    row_mean = column[1]
+    row_mean = jnp.concatenate([row_mean, row_mean], axis=1)
+    inverse = jnp.concatenate([column[0], column[0]], axis=1)
+    for jj in range(blocks // 2):
+        at = slice(256 * jj, 256 * jj + 256)
+        normed_grad = jnp.zeros((res_ref.shape[0], 256), F32)
+        for g in range(2):
+            weights = wbuf[g, :2, :, at].reshape(2 * rows_w, 256)
+            term = dot_nn(turned[:, 2 * rows_w * g : 2 * rows_w * (g + 1)], weights)
+            normed_grad = normed_grad + term.astype(BF16).astype(F32)
+        feature_grad = normed_grad * pair(gain_ref, first_block + 2 * jj)
+        unit = res_ref[:, at].astype(F32) * inverse
+        rg_ref[:, at] = (
+            og_ref[:, at].astype(F32) + inverse * (feature_grad - unit * row_mean)
+        ).astype(BF16)
+
+    y_copy.wait_recv()
+    y_sum[...] = (
+        core_sum[:, pl.ds(quarter * y, quarter)].astype(F32) + y_in[...].astype(F32)
+    ).astype(BF16)
+    z_copies = []
+    for o in (1, 2, 3):
+        begin = quarter * z_near[o] // 4
+        z_copies.append(remote(y_sum.at[:, pl.ds(begin, window)], z_in.at[o - 1], to_z[o]))
+        send(z_copies[-1])
+    own_begin = quarter * z // 4
+    summed = y_sum[:, pl.ds(own_begin, window)].astype(F32)
+    for o in (1, 2, 3):
+        z_copies[o - 1].wait_recv()
+        summed = summed + z_in[o - 1].astype(F32)
+    flat = summed.astype(BF16).reshape(2 * window * 16, 128)
+    restored = dot_nn(flat, had[:128, :128]).reshape(2, window, 16, 128)
+    base = half * core + quarter * y + own_begin
+    for i in range(window):
+        unit_at = base + i
+        bits = sign_ref[first_block + unit_at // per_block]
+        exponent = exp_ref[unit_at % per_block // groups]
+        factor = lax.shift_left(jnp.int32(1), 30 - exponent).astype(F32) * (
+            2.0**-30 / n_dp / math.sqrt(128.0)
+        )
+        turn = (2 * bits - 1).astype(F32) * factor
+        for g in range(2):
+            share[g, i] = (restored[g, i] * turn).astype(BF16)
+
+    x_copy = remote(share.at[other], slots.at[me, side], to_x)
+    send(x_copy)
+    slots[me, side] = share[side]
+    x_copy.wait_recv()
+    z_copies, y_copies, c_copies = ([], [], [])
+    for o in (1, 2, 3):
+        z_copies.append(remote(slots.at[me], slots.at[me], to_z[o]))
+        send(z_copies[-1])
+    for o in range(4):
+        slot = z_near[o] * 4 + y * 2 + core
+        if o:
+            z_copies[o - 1].wait_recv()
+        y_copies.append(remote(slots.at[slot], slots.at[slot], to_y))
+        send(y_copies[-1])
+        c_copies.append(remote(slots.at[slot], slots.at[slot], to_core))
+        send(c_copies[-1])
+    for o in range(4):
+        slot = z_near[o] * 4 + (1 - y) * 2 + core
+        y_copies[o].wait_recv()
+        c_copies.append(remote(slots.at[slot], slots.at[slot], to_core))
+        send(c_copies[-1])
+    for copy in c_copies:
+        copy.wait_recv()
+    for slot in range(n_dp):
+        zz, yy, cc = (slot // 4, slot // 2 % 2, slot % 2)
+        for i in range(window):
+            if zz < 3 and starts[zz] + i >= starts[zz + 1]:
+                continue
+            unit_at = half * cc + quarter * yy + starts[zz] + i
+            block, rest = divmod(unit_at, per_block)
+            k, group = divmod(rest, groups)
+            for fh in range(2):
+                lane = (fh * blocks + block) * 128
+                out_ref[k, 16 * group : 16 * group + 16, lane : lane + 128] = slots[slot, fh, i]
+    for copy in started:
+        copy.wait_send()
+
+
+COPIES = 30
+
+
+def fused(n_dp, residual, out_grad, ffn_weights, norm_gain, exponents, sign_bits):
+    tokens, cols = residual.shape
+    bucket = ffn_weights.shape[1]
+    blocks, groups = (cols // 128, bucket // 16)
+    units = blocks * 3 * groups
+    quarter = units // 4
+    starts = [quarter * zz // 4 for zz in range(4)]
+    window = -(-quarter // 4)
+    vmem = pl.BlockSpec(memory_space=pltpu.VMEM)
+    unit = (16, 128)
+    scratch = [
+        pltpu.VMEM((256, 256), BF16),
+        pltpu.VMEM((tokens, cols), BF16),
+        pltpu.VMEM((2, tokens, 128), F32),
+        pltpu.VMEM((2, 3, bucket, cols), BF16),
+        pltpu.VMEM((8, tokens), F32),
+        pltpu.VMEM((8, tokens), F32),
+        pltpu.VMEM((2, 3 * bucket, tokens), F32),
+        pltpu.VMEM((2, 3 * bucket, tokens), BF16),
+        pltpu.VMEM((2, 3 * bucket, tokens), BF16),
+        pltpu.VMEM((2, units) + unit, BF16),
+        pltpu.VMEM((2, units // 2) + unit, BF16),
+        pltpu.VMEM((2, units // 2) + unit, BF16),
+        pltpu.VMEM((2, quarter) + unit, BF16),
+        pltpu.VMEM((2, quarter) + unit, BF16),
+        pltpu.VMEM((3, 2, window) + unit, BF16),
+        pltpu.VMEM((2, window) + unit, BF16),
+        pltpu.VMEM((n_dp, 2, window) + unit, BF16),
+        pltpu.SemaphoreType.DMA,
+        pltpu.SemaphoreType.DMA((COPIES,)),
+        pltpu.SemaphoreType.DMA((COPIES,)),
+    ]
+    return pl.pallas_call(
+        functools.partial(kernel, (n_dp, blocks, groups, window, starts)),
+        out_shape=(
+            jax.ShapeDtypeStruct((tokens, cols), BF16),
+            jax.ShapeDtypeStruct(ffn_weights.shape, BF16),
+        ),
+        in_specs=[
+            vmem,
+            vmem,
+            pl.BlockSpec(memory_space=pl.ANY),
+            vmem,
+            pl.BlockSpec(memory_space=pltpu.SMEM),
+            vmem,
+        ],
+        out_specs=(vmem, vmem),
+        scratch_shapes=scratch,
+        compiler_params=pltpu.CompilerParams(
+            collective_id=0, has_side_effects=True, vmem_limit_bytes=48 * 2**20
+        ),
+    )(
+        residual,
+        out_grad,
+        ffn_weights,
+        norm_gain.reshape(-1, 1, 128),
+        exponents,
+        sign_bits.reshape(-1, 1, 128),
+    )
 
 
 def hadamard():
@@ -94,10 +468,19 @@
     return (resid_grad, weight_grads)
 
 
+def dispatch(n_dp, n_mp, *args):
+    cols = args[0].shape[1]
+    bucket = args[2].shape[1]
+    whole = cols % 256 == 0 and bucket % 32 == 0 and cols // 128 * 3 * (bucket // 16) % 4 == 0
+    if n_dp == 16 and n_mp == 2 and whole:
+        return fused(n_dp, *args)
+    return per_device(*args)
+
+
 def solution(mesh):
     placed = (P("dp", "mp"), P("dp", "mp"), P(None, "mp", None), P(), P(), P())
     return jax.shard_map(
-        per_device,
+        functools.partial(dispatch, mesh.shape["dp"], mesh.shape["mp"]),
         mesh=mesh,
         in_specs=placed,
         out_specs=(P("dp", "mp"), P(None, "mp", None)),

time: 257 us -> 56.3 us (0.22)
  waiting for transfers between devices: 187 us -> 0 us
  Pallas kernels: 0 us -> 47.5 us
  blocking collectives: 23.8 us -> 0 us
  between operations: 14 us -> 0.66 us
  matrix products: 13.2 us -> 0 us
  other arithmetic: 8.74 us -> 0 us
    all_gather x2 -> x0, waiting for transfers between devices: 72.8 us -> none  [the longest x1 39 us: per_device(): lax.all_gather(residual, 'mp', axis=1, tiled=True)]
    unnamed x5 -> x0, waiting for transfers between devices: 59.9 us -> none
    psum x1 -> x0, waiting for transfers between devices: 54.1 us -> none  [per_device(): lax.psum(partial_value.astype(jnp.bfloat16), 'mp').astype(jnp.float32)]
    pallas_call x0 -> x1, Pallas kernels: none -> 47.5 us  [fused(): pl.pallas_call(functools.partial(kernel, (n_dp, blocks, groups, window, s...]
    all_gather x1 -> x0, blocking collectives: 23.8 us -> none  [per_device(): gathered = lax.all_gather(own_share, 'dp', axis=0, tiled=True)]
    dot_general x7 -> x0, matrix products: 13.2 us -> none  [the longest x1 2.55 us: per_device(): lax.dot_general(hidden, grads_in, (((0,), (0,)), ((), ())), preferred_ele...]
    unnamed x32 -> x10, local copies, waits for them, and re-layouts: 0.61 us -> 6.28 us
    reduce_sum x2 -> x0, other arithmetic: 5.07 us -> none  [the longest x1 2.71 us: per_device(): jnp.sum(feature_grad * unit_rows, axis=1, keepdims=True) / feature_count]
  transfers between devices with their start and end apart: 4 -> 0, of which waited for: 4 -> 0; matrix products, arithmetic and copies ran while one was open for 9% -> 0% of each run, Pallas kernels for 0% -> 0%
where the time goes in v1:
time: 56.3 us; the launch traced here: 55.9 us
  Pallas kernels  47.5 us (84%)
  local copies, waits for them, and re-layouts  7.78 us (14%)
  between operations  0.66 us (1%)
    pallas_call x1, Pallas kernels, fused(): pl.pallas_call(functools.partial(kernel, (n_dp, blocks, groups, window, s...  47.5 us
    unnamed x10, local copies, waits for them, and re-layouts  6.28 us

profile of v1, /device:TPU:1, one launch (start us, length us, event | category | flops | bytes accessed | tf_op | source)
XLA Modules:
  0.0 55.9 jit_solution(17220519181217082696)
XLA Ops:
  0.6 0.7 %reshape.10.gain_ref = f32[36,1,128]{2,1,0:T(1,128)S(1)} reshape(f32[4608]{0:T(1024)} %param.9) | data formatting | bytes 36864 | tf_op jit(solution)/shard_map/reshape | solution.py:377
  1.4 0.7 %reshape.11.sign_ref = s32[36,1,128]{2,1,0:T(1,128)S(1)} reshape(s32[4608]{0:T(1024)} %param.11) | data formatting | bytes 36864 | tf_op jit(solution)/shard_map/reshape | solution.py:379
  2.1 0.0 copy-start
  2.1 1.3 %copy-done = bf16[256,2304]{1,0:T(8,128)(2,1)S(1)} copy-done((bf16[256,2304]{1,0:T(8,128)(2,1)S(1)}, bf16[256,2304]{1,0:T(8,128)(2,1)}, u32[]{:S(2)}) %copy-start) | copy-done | bytes 1179672
  3.4 0.0 copy-start.1
  3.4 1.3 %copy-done.1 = bf16[256,2304]{1,0:T(8,128)(2,1)S(1)} copy-done((bf16[256,2304]{1,0:T(8,128)(2,1)S(1)}, bf16[256,2304]{1,0:T(8,128)(2,1)}, u32[]{:S(2)}) %copy-start.1) | copy-done | bytes 1179672
  4.7 0.0 copy-start.2
  4.7 1.2 %copy-done.2 = bf16[3,32,4608]{2,1,0:T(8,128)(2,1)S(1)} copy-done((bf16[3,32,4608]{2,1,0:T(8,128)(2,1)S(1)}, bf16[3,32,4608]{2,1,0:T(8,128)(2,1)}, u32[]{:S(2)}) %copy-start.2) | copy-done | bytes 884760
  5.8 0.0 copy-start.3
  5.8 0.7 %copy-done.3 = s32[3]{0:T(128)S(1)} copy-done((s32[3]{0:T(128)S(1)}, s32[3]{0:T(128)}, u32[]{:S(2)}) %copy-start.3) | copy-done | bytes 36
  6.5 47.5 %shard_map.77 = (bf16[256,2304]{1,0:T(8,128)(2,1)S(1)}, bf16[3,32,4608]{2,1,0:T(8,128)(2,1)S(1)}) custom-call(bf16[256,2304]{1,0:T(8,128)(2,1)S(1)} %copy-done, bf16[256,2304]{1,0:T(8,128)(2,1)S(1)} %copy-done.1, bf16[3,32,4608]{2,1,0:T(8,128)(2,1)S(1)} %copy-done.2, f32[36,1,128]{2,1,0:T(1,128)S(1)} %reshape.10.gain_ref, s32[3]{0:T(128)S(1)} %copy-done.3, ...), custom_call_target="tpu_custom_call" | custom-call | tf_op jit(solution)/shard_map/pallas_call | solution.py:354
  54.0 1.0 %copy.10 = bf16[256,2304]{1,0:T(8,128)(2,1)} copy(bf16[256,2304]{1,0:T(8,128)(2,1)S(1)} %get-tuple-element.4) | data formatting | bytes 2359296
  55.0 0.9 %copy.11 = bf16[3,32,4608]{2,1,0:T(8,128)(2,1)} copy(bf16[3,32,4608]{2,1,0:T(8,128)(2,1)S(1)} %get-tuple-element.5) | data formatting | bytes 1769472
Async XLA Ops:
  2.1 1.3 %copy-start = (bf16[256,2304]{1,0:T(8,128)(2,1)S(1)}, bf16[256,2304]{1,0:T(8,128)(2,1)}, u32[]{:S(2)}) copy-start(bf16[256,2304]{1,0:T(8,128)(2,1)} %res_ref.1) | copy-start | bytes 3538948
  3.4 1.3 %copy-start.1 = (bf16[256,2304]{1,0:T(8,128)(2,1)S(1)}, bf16[256,2304]{1,0:T(8,128)(2,1)}, u32[]{:S(2)}) copy-start(bf16[256,2304]{1,0:T(8,128)(2,1)} %og_ref.1) | copy-start | bytes 3538948
  4.7 1.2 %copy-start.2 = (bf16[3,32,4608]{2,1,0:T(8,128)(2,1)S(1)}, bf16[3,32,4608]{2,1,0:T(8,128)(2,1)}, u32[]{:S(2)}) copy-start(bf16[3,32,4608]{2,1,0:T(8,128)(2,1)} %w_ref.1) | copy-start | bytes 2654212
  5.8 0.7 %copy-start.3 = (s32[3]{0:T(128)S(1)}, s32[3]{0:T(128)}, u32[]{:S(2)}) copy-start(s32[3]{0:T(128)} %exp_ref.1) | copy-start | bytes 40

commit v2 on v1

v2 whole, which is shorter than its diff:
```python
import functools
import math

import jax
import jax.numpy as jnp
from jax import lax
from jax.experimental import pallas as pl
from jax.experimental.pallas import tpu as pltpu
from jax.sharding import PartitionSpec as P

MESH = pl.DeviceIdType.MESH
F32 = jnp.float32
BF16 = jnp.bfloat16


def dot_nt(left, right):
    return lax.dot_general(left, right, (((1,), (1,)), ((), ())), preferred_element_type=F32)


def dot_nn(left, right):
    return lax.dot_general(left, right, (((1,), (0,)), ((), ())), preferred_element_type=F32)


def split_dot(dot, left, right, split_left):
    wide = left if split_left else right
    high = wide.astype(BF16)
    low = (wide - high.astype(F32)).astype(BF16)
    if split_left:
        return dot(high, right) + dot(low, right)
    return dot(left, high) + dot(left, low)


def signs_256():
    rows = lax.broadcasted_iota(jnp.int32, (256, 256), 0)
    cols = lax.broadcasted_iota(jnp.int32, (256, 256), 1)
    anded = jnp.bitwise_and(jnp.bitwise_and(rows, cols), 127)
    for shift in (4, 2, 1):
        anded = jnp.bitwise_xor(anded, jnp.right_shift(anded, shift))
    value = 1 - 2 * jnp.bitwise_and(anded, 1)
    same = jnp.right_shift(rows, 7) == jnp.right_shift(cols, 7)
    return jnp.where(same, value, 0).astype(F32).astype(BF16)


def to_column(row):
    return jnp.broadcast_to(row[0:1], (128, row.shape[1])).T


def pair(ref, first):
    return jnp.concatenate([ref[pl.ds(first, 1)], ref[pl.ds(first + 1, 1)]], axis=1)


def kernel(
    sizes,
    res_hbm,
    og_hbm,
    w_ref,
    gain_in,
    exp_ref,
    sign_in,
    rg_ref,
    out_ref,
    res_ref,
    og_ref,
    gain_ref,
    sign_ref,
    had,
    normed,
    column,
    wbuf,
    sq_mine,
    sq_peer,
    part,
    part_out,
    part_in,
    *rest,
):
    n_dp, blocks, groups, chunks = sizes
    buffers = rest[:-3]
    local_sem, send_sem, recv_sem = rest[-3:]
    kinds = len(buffers) // len(chunks)
    cols = blocks * 128
    rows_w = 16 * groups
    split = groups // 2
    per_pair = 3 * split
    me = lax.axis_index("dp")
    side = lax.axis_index("mp")
    other = 1 - side
    core = me % 2
    y = (me // 2) % 2
    z = me // 4
    z_near = [z, z + 1 - 2 * (z % 2), (z + 2) % 4, 3 - z]
    first_block = side * blocks
    to_x = (me, other)
    to_core = (me + 1 - 2 * core, side)
    to_y = (me + 2 - 4 * y, side)
    to_z = [None] + [(zz * 4 + y * 2 + core, side) for zz in z_near[1:]]
    started = []

    def send(src, dst, target):
        index = len(started)
        copy = pltpu.make_async_remote_copy(
            src_ref=src,
            dst_ref=dst,
            send_sem=send_sem.at[index],
            recv_sem=recv_sem.at[index],
            device_id=target,
            device_id_type=MESH,
        )
        copy.start()
        started.append(copy)
        return copy

    barrier = pltpu.get_barrier_semaphore()
    partners = [to_x, to_core, to_y] + to_z[1:]
    for target in partners:
        pl.semaphore_signal(barrier, inc=1, device_id=target, device_id_type=MESH)

    own_cols = pl.ds(pl.multiple_of(side * cols, 128), cols)
    peer_cols = pl.ds(pl.multiple_of(other * cols, 128), cols)
    get_res = pltpu.make_async_copy(res_hbm, res_ref, local_sem.at[0])
    get_res.start()
    get_og = pltpu.make_async_copy(og_hbm, og_ref, local_sem.at[1])
    get_og.start()
    get_w = pltpu.make_async_copy(w_ref.at[:, :, own_cols], wbuf.at[side], local_sem.at[2])
    get_w.start()
    had[...] = signs_256()
    gain_ref[...] = gain_in[...]
    sign_ref[...] = (2 * sign_in[...] - 1).astype(F32)
    get_res.wait()
    wide = res_ref[...].astype(F32)
    ones = jnp.ones((8, cols), BF16)
    sq_mine[...] = split_dot(dot_nt, ones, wide * wide, False)
    pl.semaphore_wait(barrier, len(partners))

    sq_copy = send(sq_mine, sq_peer, to_x)
    core_rows = pl.ds(pl.multiple_of(core * (rows_w // 2), 16), rows_w // 2)
    w_copies = {}
    for k in (2, 0, 1):
        w_copies[k] = send(
            w_ref.at[k, core_rows, peer_cols], wbuf.at[side, k, core_rows], to_x
        )

    get_og.wait()
    get_w.wait()
    part[side, 2 * rows_w : 3 * rows_w] = dot_nt(wbuf[side, 2], og_ref[...])
    sq_copy.wait_recv()
    total_sq = sq_mine[...] + sq_peer[...]
    inverse = to_column(lax.rsqrt(total_sq / float(2 * cols) + 1e-06))
    column[0] = inverse
    for j in range(blocks):
        at = slice(128 * j, 128 * j + 128)
        unit = res_ref[:, at].astype(F32) * inverse
        normed[:, at] = (unit * gain_ref[pl.ds(first_block + j, 1)]).astype(BF16)
    part[side, : 2 * rows_w] = dot_nt(
        wbuf[side, :2].reshape(2 * rows_w, cols), normed[...]
    )
    part_out[side] = part[side].astype(BF16)
    own_part = send(part_out.at[side], part_in.at[side], to_x)

    shared = {}
    for k in (2, 0, 1):
        w_copies[k].wait_recv()
        landed = wbuf.at[other, k, core_rows]
        shared[k] = send(landed, landed, to_core)
    shared[2].wait_recv()
    part[other, 2 * rows_w : 3 * rows_w] = dot_nt(wbuf[other, 2], og_ref[...])
    shared[0].wait_recv()
    shared[1].wait_recv()
    part[other, : 2 * rows_w] = dot_nt(
        wbuf[other, :2].reshape(2 * rows_w, cols), normed[...]
    )
    part_out[other] = part[other].astype(BF16)
    peer_part = send(part_out.at[other], part_in.at[other], to_x)
    own_part.wait_recv()
    peer_part.wait_recv()

    pair_grads = []
    hiddens = []
    row_total = jnp.zeros((1, part.shape[2]), F32)
    for g in range(2):
        full = part[g] + part_in[g].astype(F32)
        gate_pre = full[:rows_w]
        up_proj = full[rows_w : 2 * rows_w]
        hidden_grad = full[2 * rows_w :]
        activated, slope = gelu_parts(gate_pre)
        hiddens.append((activated * up_proj).astype(BF16))
        gate_grad = (hidden_grad * up_proj * slope).astype(BF16)
        up_grad = (hidden_grad * activated).astype(BF16)
        pair_grads += [gate_grad, up_grad]
        row_total = row_total + jnp.sum(
            gate_grad.astype(F32) * gate_pre + up_grad.astype(F32) * up_proj,
            axis=0,
            keepdims=True,
        )
    pair_grad = jnp.concatenate(pair_grads, axis=0)
    hidden = jnp.concatenate(hiddens, axis=0)

    scales = [
        lax.shift_left(jnp.int32(1), exp_ref[k]).astype(F32) * (1.0 / math.sqrt(128.0))
        for k in range(3)
    ]
    order = [(0, 0), (0, 1), (1, 0), (1, 1), (0, 2), (1, 2)]

    class Chunk:
        pass

    lanes = []
    for q, (first_pair, pairs, window, starts) in enumerate(chunks):
        chunk = Chunk()
        lanes.append(chunk)
        chunk.first, chunk.pairs, chunk.window, chunk.starts = (
            first_pair,
            pairs,
            window,
            starts,
        )
        chunk.units = pairs * per_pair
        (
            chunk.terms,
            chunk.core_in,
            chunk.core_sum,
            chunk.y_in,
            chunk.y_sum,
            chunk.z_in,
            chunk.share,
            chunk.slots,
        ) = buffers[q * kinds : (q + 1) * kinds]

    def make_terms(chunk):
        table = had[...]
        for jj in range(chunk.first, chunk.first + chunk.pairs):
            at = slice(256 * jj, 256 * jj + 256)
            grads = jnp.concatenate(
                [dot_nn(pair_grad, normed[:, at]), dot_nn(hidden, og_ref[:, at])], axis=0
            )
            signed = grads * pair(sign_ref, first_block + 2 * jj)
            rotated = split_dot(dot_nn, signed, table, True)
            for index, (g, k) in enumerate(order):
                piece = rotated[index * rows_w : (index + 1) * rows_w] * scales[k]
                piece = jnp.clip(piece, -127.0, 127.0).astype(BF16)
                for b in range(2):
                    for i in range(groups):
                        unit_at = (jj - chunk.first) * per_pair + k * split + i % split
                        chunk.terms[i // split, b, g, unit_at] = piece[
                            16 * i : 16 * i + 16, 128 * b : 128 * b + 128
                        ]
        chunk.core_copy = send(chunk.terms.at[1 - core], chunk.core_in, to_core)

    def after_core(chunk):
        chunk.core_copy.wait_recv()
        chunk.core_sum[...] = (
            chunk.terms[core].astype(F32) + chunk.core_in[...].astype(F32)
        ).astype(BF16)
        chunk.y_copy = send(chunk.core_sum.at[1 - y], chunk.y_in, to_y)

    def after_y(chunk):
        chunk.y_copy.wait_recv()
        chunk.y_sum[...] = (
            chunk.core_sum[y].astype(F32) + chunk.y_in[...].astype(F32)
        ).astype(BF16)
        chunk.z_copies = []
        for o in (1, 2, 3):
            begin = chunk.units * z_near[o] // 4
            chunk.z_copies.append(
                send(chunk.y_sum.at[:, pl.ds(begin, chunk.window)], chunk.z_in.at[o - 1], to_z[o])
            )

    def after_z(chunk):
        window = chunk.window
        begin = chunk.units * z // 4
        summed = chunk.y_sum[:, pl.ds(begin, window)].astype(F32)
        for o in (1, 2, 3):
            chunk.z_copies[o - 1].wait_recv()
            summed = summed + chunk.z_in[o - 1].astype(F32)
        flat = summed.astype(BF16).reshape(2 * window * 16, 128)
        restored = dot_nn(flat, had[:128, :128]).reshape(2, window, 16, 128)
        for i in range(window):
            unit_at = begin + i
            block = 2 * (chunk.first + unit_at // per_pair) + y
            exponent = exp_ref[unit_at % per_pair // split]
            factor = lax.shift_left(jnp.int32(1), 30 - exponent).astype(F32) * (
                2.0**-30 / n_dp / math.sqrt(128.0)
            )
            turn = sign_ref[pl.ds(first_block + block, 1)] * factor
            for g in range(2):
                chunk.share[g, i] = (restored[g, i] * turn).astype(BF16)
        chunk.x_copy = send(chunk.share.at[other], chunk.slots.at[me, side], to_x)
        chunk.slots[me, side] = chunk.share[side]

    def forward(chunk, slot, targets):
        block = chunk.slots.at[slot]
        return [send(block, block, target) for target in targets]

    def after_x(chunk):
        chunk.x_copy.wait_recv()
        chunk.z_copies = forward(chunk, me, to_z[1:])
        to_both = forward(chunk, me, [to_y, to_core])
        chunk.y_copies = to_both[:1]
        chunk.c_copies = to_both[1:]

    def gather_z(chunk):
        for o in (1, 2, 3):
            chunk.z_copies[o - 1].wait_recv()
            to_both = forward(chunk, z_near[o] * 4 + y * 2 + core, [to_y, to_core])
            chunk.y_copies.append(to_both[0])
            chunk.c_copies.append(to_both[1])

    def gather_y(chunk):
        for o in range(4):
            chunk.y_copies[o].wait_recv()
            chunk.c_copies += forward(
                chunk, z_near[o] * 4 + (1 - y) * 2 + core, [to_core]
            )

    def assemble(chunk):
        for copy in chunk.c_copies:
            copy.wait_recv()
        for slot in range(n_dp):
            zz, yy, cc = (slot // 4, slot // 2 % 2, slot % 2)
            for i in range(chunk.window):
                unit_at = chunk.starts[zz] + i
                if zz < 3 and unit_at >= chunk.starts[zz + 1]:
                    continue
                pair_at, rest_at = divmod(unit_at, per_pair)
                block = 2 * (chunk.first + pair_at) + yy
                k = rest_at // split
                top = 16 * (cc * split + rest_at % split)
                for fh in range(2):
                    lane = (fh * blocks + block) * 128
                    out_ref[k, top : top + 16, lane : lane + 128] = chunk.slots[slot, fh, i]

    def make_resid(first_pair, last_pair):
        row_mean = jnp.concatenate([column[1], column[1]], axis=1)
        inverse = jnp.concatenate([column[0], column[0]], axis=1)
        for jj in range(first_pair, last_pair):
            at = slice(256 * jj, 256 * jj + 256)
            normed_grad = jnp.zeros((res_ref.shape[0], 256), F32)
            for g in range(2):
                weights = wbuf[g, :2, :, at].reshape(2 * rows_w, 256)
                term = dot_nn(turned[:, 2 * rows_w * g : 2 * rows_w * (g + 1)], weights)
                normed_grad = normed_grad + term.astype(BF16).astype(F32)
            feature_grad = normed_grad * pair(gain_ref, first_block + 2 * jj)
            unit = res_ref[:, at].astype(F32) * inverse
            rg_ref[:, at] = (
                og_ref[:, at].astype(F32) + inverse * (feature_grad - unit * row_mean)
            ).astype(BF16)

    one, two = lanes
    all_pairs = blocks // 2
    make_terms(one)
    make_terms(two)
    after_core(one)
    column[1] = to_column(row_total / float(2 * cols))
    turned = pair_grad.astype(F32).T.astype(BF16)
    after_core(two)
    make_resid(0, all_pairs // 3)
    after_y(one)
    make_resid(all_pairs // 3, 2 * all_pairs // 3)
    after_y(two)
    after_z(one)
    make_resid(2 * all_pairs // 3, all_pairs)
    after_x(one)
    after_z(two)
    gather_z(one)
    after_x(two)
    gather_y(one)
    gather_z(two)
    gather_y(two)
    assemble(one)
    assemble(two)
    for copy in started:
        copy.wait_send()


COPIES = 9 + 2 * 21


def fused(n_dp, residual, out_grad, ffn_weights, norm_gain, exponents, sign_bits):
    tokens, cols = residual.shape
    bucket = ffn_weights.shape[1]
    blocks, groups = (cols // 128, bucket // 16)
    all_pairs = blocks // 2
    per_pair = 3 * groups // 2
    cut = all_pairs // 2
    vmem = pl.BlockSpec(memory_space=pltpu.VMEM)
    hbm = pl.BlockSpec(memory_space=pltpu.HBM)
    scratch = [
        pltpu.VMEM((tokens, cols), BF16),
        pltpu.VMEM((tokens, cols), BF16),
        pltpu.VMEM((2 * blocks, 128), F32),
        pltpu.VMEM((2 * blocks, 128), F32),
        pltpu.VMEM((256, 256), BF16),
        pltpu.VMEM((tokens, cols), BF16),
        pltpu.VMEM((2, tokens, 128), F32),
        pltpu.VMEM((2, 3, bucket, cols), BF16),
        pltpu.VMEM((8, tokens), F32),
        pltpu.VMEM((8, tokens), F32),
        pltpu.VMEM((2, 3 * bucket, tokens), F32),
        pltpu.VMEM((2, 3 * bucket, tokens), BF16),
        pltpu.VMEM((2, 3 * bucket, tokens), BF16),
    ]
    chunks = []
    for first, pairs in ((0, cut), (cut, all_pairs - cut)):
        units = pairs * per_pair
        window = -(-units // 4)
        chunks.append((first, pairs, window, [units * zz // 4 for zz in range(4)]))
        for lead in (
            (2, 2, 2, units),
            (2, 2, units),
            (2, 2, units),
            (2, units),
            (2, units),
            (3, 2, window),
            (2, window),
            (n_dp, 2, window),
        ):
            scratch.append(pltpu.VMEM(lead + (16, 128), BF16))
    scratch += [
        pltpu.SemaphoreType.DMA((3,)),
        pltpu.SemaphoreType.DMA((COPIES,)),
        pltpu.SemaphoreType.DMA((COPIES,)),
    ]
    return pl.pallas_call(
        functools.partial(kernel, (n_dp, blocks, groups, chunks)),
        out_shape=(
            pltpu.VMEM((tokens, cols), BF16),
            pltpu.VMEM(ffn_weights.shape, BF16),
        ),
        in_specs=[
            hbm,
            hbm,
            hbm,
            vmem,
            pl.BlockSpec(memory_space=pltpu.SMEM),
            vmem,
        ],
        out_specs=(vmem, vmem),
        scratch_shapes=scratch,
        compiler_params=pltpu.CompilerParams(
            collective_id=0, has_side_effects=True, vmem_limit_bytes=58 * 2**20
        ),
    )(
        residual,
        out_grad,
        ffn_weights,
        norm_gain.reshape(-1, 128),
        exponents,
        sign_bits.reshape(-1, 128),
    )


def hadamard():
    indices = jnp.arange(128, dtype=jnp.int32)
    anded = jnp.bitwise_and(indices[:, None], indices[None, :])
    parity = jnp.zeros((128, 128), jnp.int32)
    for offset in range(7):
        parity = parity + jnp.bitwise_and(jnp.right_shift(anded, offset), 1)
    return (1 - 2 * (parity % 2)).astype(jnp.float32) / math.sqrt(128.0)


def gelu_parts(values):
    tanh_input = 0.7978845608 * (values + 0.044715 * values * values * values)
    tanhed = jnp.tanh(tanh_input)
    forward = 0.5 * values * (1.0 + tanhed)
    gelu_slope = 0.5 * (1.0 + tanhed) + 0.5 * values * (1.0 - tanhed * tanhed) * 0.7978845608 * (
        1.0 + 3.0 * 0.044715 * values * values
    )
    return (forward, gelu_slope)


def restore(summed, factors, sign_table, hadamard_table):
    block_count = sign_table.shape[0]
    widened = lax.optimization_barrier(summed).astype(jnp.float32).reshape(3, -1, block_count, 128)
    scaled = widened * factors[:, None, None, None]
    restored = (
        jnp.einsum("kubj,jc->kubc", scaled, hadamard_table, precision=lax.Precision.HIGHEST)
        * sign_table
    )
    return restored.astype(jnp.bfloat16).reshape(3, -1, block_count * 128)


def per_device(residual, out_grad, ffn_weights, norm_gain, exponents, sign_bits):
    full_rows, grads_in = (
        lax.all_gather(residual, "mp", axis=1, tiled=True),
        lax.all_gather(out_grad, "mp", axis=1, tiled=True),
    )
    feature_count = full_rows.shape[1]
    col_count = residual.shape[1]
    col_start = lax.axis_index("mp") * col_count
    bucket_rows = ffn_weights.shape[1]
    rows_wide = full_rows.astype(jnp.float32)
    inverse = lax.rsqrt(jnp.mean(rows_wide * rows_wide, axis=1, keepdims=True) + 1e-06)
    unit_rows = rows_wide * inverse
    normed = (unit_rows * norm_gain).astype(jnp.bfloat16)
    pair_weights = ffn_weights[:2]
    gate_up = jnp.einsum("td,khd->tkh", normed, pair_weights, preferred_element_type=jnp.float32)
    gate_pre = gate_up[:, 0]
    up_proj = gate_up[:, 1]
    activated, gelu_slope = gelu_parts(gate_pre)
    hidden = (activated * up_proj).astype(jnp.bfloat16)
    hidden_grad = lax.dot_general(
        grads_in, ffn_weights[2], (((1,), (1,)), ((), ())), preferred_element_type=jnp.float32
    )
    gate_grad = (hidden_grad * up_proj * gelu_slope).astype(jnp.bfloat16)
    up_grad = (hidden_grad * activated).astype(jnp.bfloat16)
    pair_grad = jnp.stack([gate_grad, up_grad], axis=1)
    partial_value = jnp.einsum(
        "tkh,khd->td", pair_grad, pair_weights, preferred_element_type=jnp.float32
    )
    own_unit = lax.dynamic_slice_in_dim(unit_rows, col_start, col_count, 1)
    normed_grad = lax.psum(partial_value.astype(jnp.bfloat16), "mp").astype(jnp.float32)
    feature_grad = normed_grad * norm_gain
    row_mean = jnp.sum(feature_grad * unit_rows, axis=1, keepdims=True) / feature_count
    own_grad = lax.dynamic_slice_in_dim(feature_grad, col_start, col_count, 1)
    resid_grad = (out_grad.astype(jnp.float32) + inverse * (own_grad - own_unit * row_mean)).astype(
        jnp.bfloat16
    )
    pair_wgrad = jnp.einsum("tkh,td->khd", pair_grad, normed, preferred_element_type=jnp.float32)
    down_wgrad = lax.dot_general(
        hidden, grads_in, (((0,), (0,)), ((), ())), preferred_element_type=jnp.float32
    )
    stacked = jnp.concatenate([pair_wgrad, down_wgrad[None]], axis=0)
    block_count = feature_count // 128
    sign_table = (2 * sign_bits - 1).astype(jnp.float32).reshape(block_count, 128)
    hadamard_table = hadamard()
    shaped = stacked.reshape(3, bucket_rows, block_count, 128) * sign_table
    rotated = jnp.einsum("kubj,jc->kubc", shaped, hadamard_table, precision=lax.Precision.HIGHEST)
    scales = jnp.exp2(exponents.astype(jnp.float32))
    quantized = jnp.clip(rotated * scales[:, None, None, None], -127.0, 127.0).astype(jnp.bfloat16)
    flat_terms = lax.optimization_barrier(quantized).astype(jnp.float32).reshape(-1, 128)
    factors = jnp.exp2(-exponents.astype(jnp.float32)) / float(lax.axis_size("dp"))
    own_share = lax.psum_scatter(flat_terms, "dp", scatter_dimension=0, tiled=True).astype(
        jnp.bfloat16
    )
    gathered = lax.all_gather(own_share, "dp", axis=0, tiled=True)
    weight_grads = restore(gathered, factors, sign_table, hadamard_table)
    return (resid_grad, weight_grads)


def dispatch(n_dp, n_mp, *args):
    cols = args[0].shape[1]
    bucket = args[2].shape[1]
    whole = cols % 256 == 0 and bucket % 32 == 0 and cols >= 512
    if n_dp == 16 and n_mp == 2 and whole:
        return fused(n_dp, *args)
    return per_device(*args)


def solution(mesh):
    placed = (P("dp", "mp"), P("dp", "mp"), P(None, "mp", None), P(), P(), P())
    return jax.shard_map(
        functools.partial(dispatch, mesh.shape["dp"], mesh.shape["mp"]),
        mesh=mesh,
        in_specs=placed,
        out_specs=(P("dp", "mp"), P(None, "mp", None)),
        check_vma=False,
    )
```

time: 56.3 us -> 49.1 us (0.87)
  local copies, waits for them, and re-layouts: 7.78 us -> 1.93 us
  Pallas kernels: 47.5 us -> 46.3 us
    unnamed x10 -> x2, local copies, waits for them, and re-layouts: 6.28 us -> 1.93 us
    reshape x2 -> x0, local copies, waits for them, and re-layouts: 1.5 us -> none  [the longest x1 0.75 us: fused(): sign_bits.reshape(-1, 1, 128)]
    pallas_call x1, Pallas kernels: 47.5 us -> 46.3 us  [fused(): pl.pallas_call(functools.partial(kernel, (n_dp, blocks, groups, chunks)),...]
where the time goes in v2:
time: 49.1 us; the launch traced here: 48.9 us
  Pallas kernels  46.3 us (94%)
  local copies, waits for them, and re-layouts  1.93 us (4%)
  between operations  0.64 us (1%)
    pallas_call x1, Pallas kernels, fused(): pl.pallas_call(functools.partial(kernel, (n_dp, blocks, groups, chunks)),...  46.3 us
    unnamed x2, local copies, waits for them, and re-layouts  1.93 us

profile of v2, /device:TPU:1, one launch (start us, length us, event | category | flops | bytes accessed | tf_op | source)
XLA Modules:
  0.0 48.9 jit_solution(6324284908905036796)
XLA Ops:
  0.6 46.3 %shard_map.77 = (bf16[256,2304]{1,0:T(8,128)(2,1)S(1)}, bf16[3,32,4608]{2,1,0:T(8,128)(2,1)S(1)}) custom-call(bf16[256,2304]{1,0:T(8,128)(2,1)} %res_hbm.1, bf16[256,2304]{1,0:T(8,128)(2,1)} %og_hbm.1, bf16[3,32,4608]{2,1,0:T(8,128)(2,1)} %w_ref.1, f32[36,128]{1,0:T(8,128)} %bitcast.2, s32[3]{0:T(128)} %exp_ref.1, s32[36,128]{1,0:T(8,128)} %bitcast.3), custom_call_target="tpu_custom_call" | custom-call | tf_op jit(solution)/shard_map/pallas_call | solution.py:423
  47.0 1.0 %copy.10 = bf16[256,2304]{1,0:T(8,128)(2,1)} copy(bf16[256,2304]{1,0:T(8,128)(2,1)S(1)} %get-tuple-element.2) | data formatting | bytes 2359296
  48.0 0.9 %copy.11 = bf16[3,32,4608]{2,1,0:T(8,128)(2,1)} copy(bf16[3,32,4608]{2,1,0:T(8,128)(2,1)S(1)} %get-tuple-element.3) | data formatting | bytes 1769472

commit v3 on v2

--- a/solution.py
+++ b/solution.py
@@ -13,21 +13,14 @@
 BF16 = jnp.bfloat16
 
 
-def dot_nt(left, right):
-    return lax.dot_general(left, right, (((1,), (1,)), ((), ())), preferred_element_type=F32)
-
-
 def dot_nn(left, right):
     return lax.dot_general(left, right, (((1,), (0,)), ((), ())), preferred_element_type=F32)
 
 
-def split_dot(dot, left, right, split_left):
-    wide = left if split_left else right
-    high = wide.astype(BF16)
-    low = (wide - high.astype(F32)).astype(BF16)
-    if split_left:
-        return dot(high, right) + dot(low, right)
-    return dot(left, high) + dot(left, low)
+def split_dot(left, right):
+    high = left.astype(BF16)
+    low = (left - high.astype(F32)).astype(BF16)
+    return dot_nn(high, right) + dot_nn(low, right)
 
 
 def signs_256():
@@ -67,6 +60,8 @@
     normed,
     column,
     wbuf,
+    og_turned,
+    normed_turned,
     sq_mine,
     sq_peer,
     part,
@@ -116,7 +111,6 @@
         pl.semaphore_signal(barrier, inc=1, device_id=target, device_id_type=MESH)
 
     own_cols = pl.ds(pl.multiple_of(side * cols, 128), cols)
-    peer_cols = pl.ds(pl.multiple_of(other * cols, 128), cols)
     get_res = pltpu.make_async_copy(res_hbm, res_ref, local_sem.at[0])
     get_res.start()
     get_og = pltpu.make_async_copy(og_hbm, og_ref, local_sem.at[1])
@@ -126,23 +120,37 @@
     had[...] = signs_256()
     gain_ref[...] = gain_in[...]
     sign_ref[...] = (2 * sign_in[...] - 1).astype(F32)
+    core_rows = pl.ds(pl.multiple_of(core * (rows_w // 2), 16), rows_w // 2)
+    pieces = 3
+    cuts = [256 * (blocks // 2 * p // pieces) for p in range(pieces + 1)]
+
+    def send_w(p):
+        width = cuts[p + 1] - cuts[p]
+        from_cols = pl.ds(pl.multiple_of(other * cols + cuts[p], 128), width)
+        return send(
+            w_ref.at[:, core_rows, from_cols],
+            wbuf.at[side, :, core_rows, pl.ds(cuts[p], width)],
+            to_x,
+        )
+
+    pl.semaphore_wait(barrier, len(partners))
+    w_copies = [send_w(0), send_w(1)]
     get_res.wait()
-    wide = res_ref[...].astype(F32)
-    ones = jnp.ones((8, cols), BF16)
-    sq_mine[...] = split_dot(dot_nt, ones, wide * wide, False)
-    pl.semaphore_wait(barrier, len(partners))
-
+    squares = jnp.zeros(column.shape[1:], F32)
+    for j in range(blocks):
+        wide = res_ref[:, 128 * j : 128 * j + 128].astype(F32)
+        squares = squares + wide * wide
+    sums = jnp.sum(squares.T, axis=0, keepdims=True)
+    sq_mine[...] = jnp.broadcast_to(sums, sq_mine.shape)
     sq_copy = send(sq_mine, sq_peer, to_x)
-    core_rows = pl.ds(pl.multiple_of(core * (rows_w // 2), 16), rows_w // 2)
-    w_copies = {}
-    for k in (2, 0, 1):
-        w_copies[k] = send(
-            w_ref.at[k, core_rows, peer_cols], wbuf.at[side, k, core_rows], to_x
-        )
+    w_copies.append(send_w(2))
 
     get_og.wait()
+    for j in range(blocks):
+        at = slice(128 * j, 128 * j + 128)
+        og_turned[at] = og_ref[:, at].T
     get_w.wait()
-    part[side, 2 * rows_w : 3 * rows_w] = dot_nt(wbuf[side, 2], og_ref[...])
+    part[side, 2 * rows_w : 3 * rows_w] = dot_nn(wbuf[side, 2], og_turned[...])
     sq_copy.wait_recv()
     total_sq = sq_mine[...] + sq_peer[...]
     inverse = to_column(lax.rsqrt(total_sq / float(2 * cols) + 1e-06))
@@ -150,25 +158,32 @@
     for j in range(blocks):
         at = slice(128 * j, 128 * j + 128)
         unit = res_ref[:, at].astype(F32) * inverse
-        normed[:, at] = (unit * gain_ref[pl.ds(first_block + j, 1)]).astype(BF16)
-    part[side, : 2 * rows_w] = dot_nt(
-        wbuf[side, :2].reshape(2 * rows_w, cols), normed[...]
+        scaled = (unit * gain_ref[pl.ds(first_block + j, 1)]).astype(BF16)
+        normed[:, at] = scaled
+        normed_turned[at] = scaled.T
+    part[side, : 2 * rows_w] = dot_nn(
+        wbuf[side, :2].reshape(2 * rows_w, cols), normed_turned[...]
     )
     part_out[side] = part[side].astype(BF16)
     own_part = send(part_out.at[side], part_in.at[side], to_x)
 
-    shared = {}
-    for k in (2, 0, 1):
-        w_copies[k].wait_recv()
-        landed = wbuf.at[other, k, core_rows]
-        shared[k] = send(landed, landed, to_core)
-    shared[2].wait_recv()
-    part[other, 2 * rows_w : 3 * rows_w] = dot_nt(wbuf[other, 2], og_ref[...])
-    shared[0].wait_recv()
-    shared[1].wait_recv()
-    part[other, : 2 * rows_w] = dot_nt(
-        wbuf[other, :2].reshape(2 * rows_w, cols), normed[...]
-    )
+    shared = []
+    pair_part = jnp.zeros((2 * rows_w, part.shape[2]), F32)
+    down_part = jnp.zeros((rows_w, part.shape[2]), F32)
+    for p in range(pieces + 1):
+        if p < pieces:
+            w_copies[p].wait_recv()
+            landed = wbuf.at[other, :, core_rows, pl.ds(cuts[p], cuts[p + 1] - cuts[p])]
+            shared.append(send(landed, landed, to_core))
+        if p > 0:
+            shared[p - 1].wait_recv()
+            width = cuts[p] - cuts[p - 1]
+            at = slice(cuts[p - 1], cuts[p])
+            weights = wbuf[other, :2, :, at].reshape(2 * rows_w, width)
+            pair_part = pair_part + dot_nn(weights, normed_turned[at])
+            down_part = down_part + dot_nn(wbuf[other, 2, :, at], og_turned[at])
+    part[other, : 2 * rows_w] = pair_part
+    part[other, 2 * rows_w : 3 * rows_w] = down_part
     part_out[other] = part[other].astype(BF16)
     peer_part = send(part_out.at[other], part_in.at[other], to_x)
     own_part.wait_recv()
@@ -234,7 +249,7 @@
                 [dot_nn(pair_grad, normed[:, at]), dot_nn(hidden, og_ref[:, at])], axis=0
             )
             signed = grads * pair(sign_ref, first_block + 2 * jj)
-            rotated = split_dot(dot_nn, signed, table, True)
+            rotated = split_dot(signed, table)
             for index, (g, k) in enumerate(order):
                 piece = rotated[index * rows_w : (index + 1) * rows_w] * scales[k]
                 piece = jnp.clip(piece, -127.0, 127.0).astype(BF16)
@@ -372,6 +387,17 @@
         copy.wait_send()
 
 
+def write_out(rg_ref, wg_ref, rg_out, wg_out, sems):
+    copies = [
+        pltpu.make_async_copy(rg_ref, rg_out, sems.at[0]),
+        pltpu.make_async_copy(wg_ref, wg_out, sems.at[1]),
+    ]
+    for copy in copies:
+        copy.start()
+    for copy in copies:
+        copy.wait()
+
+
 COPIES = 9 + 2 * 21
 
 
@@ -393,6 +419,8 @@
         pltpu.VMEM((tokens, cols), BF16),
         pltpu.VMEM((2, tokens, 128), F32),
         pltpu.VMEM((2, 3, bucket, cols), BF16),
+        pltpu.VMEM((cols, tokens), BF16),
+        pltpu.VMEM((cols, tokens), BF16),
         pltpu.VMEM((8, tokens), F32),
         pltpu.VMEM((8, tokens), F32),
         pltpu.VMEM((2, 3 * bucket, tokens), F32),
@@ -420,7 +448,7 @@
         pltpu.SemaphoreType.DMA((COPIES,)),
         pltpu.SemaphoreType.DMA((COPIES,)),
     ]
-    return pl.pallas_call(
+    results = pl.pallas_call(
         functools.partial(kernel, (n_dp, blocks, groups, chunks)),
         out_shape=(
             pltpu.VMEM((tokens, cols), BF16),
@@ -447,6 +475,13 @@
         exponents,
         sign_bits.reshape(-1, 128),
     )
+    return pl.pallas_call(
+        write_out,
+        out_shape=[jax.ShapeDtypeStruct(result.shape, BF16) for result in results],
+        in_specs=[vmem, vmem],
+        out_specs=[hbm, hbm],
+        scratch_shapes=[pltpu.SemaphoreType.DMA((2,))],
+    )(*results)
 
 
 def hadamard():

time: 49.1 us -> 50.5 us (1.029)
  Pallas kernels: 46.3 us -> 47.7 us
    pallas_call x0 -> x1, Pallas kernels: none -> 2.84 us  [fused(): pl.pallas_call(write_out, out_shape=[jax.ShapeDtypeStruct(result.shape, B...]
    pallas_call x1, Pallas kernels: 46.3 us -> 44.8 us  [fused(): pl.pallas_call(functools.partial(kernel, (n_dp, blocks, groups, chunks)),...]
    unnamed x2 -> x4, local copies, waits for them, and re-layouts: 1.93 us -> 1.99 us
where the time goes in v3:
time: 50.5 us; the launch traced here: 50.3 us
  Pallas kernels  47.7 us (94%)
  local copies, waits for them, and re-layouts  1.99 us (4%)
  between operations  0.65 us (1%)
    pallas_call x1, Pallas kernels, fused(): pl.pallas_call(functools.partial(kernel, (n_dp, blocks, groups, chunks)),...  44.8 us
    pallas_call x1, Pallas kernels, fused(): pl.pallas_call(write_out, out_shape=[jax.ShapeDtypeStruct(result.shape, B...  2.84 us
    unnamed x4, local copies, waits for them, and re-layouts  1.99 us

profile of v3, /device:TPU:1, one launch (start us, length us, event | category | flops | bytes accessed | tf_op | source)
XLA Modules:
  0.0 50.3 jit_solution(9339302715848512619)
XLA Ops:
  0.6 44.8 %shard_map.77 = (bf16[256,2304]{1,0:T(8,128)(2,1)S(1)}, bf16[3,32,4608]{2,1,0:T(8,128)(2,1)S(1)}) custom-call(bf16[256,2304]{1,0:T(8,128)(2,1)} %res_hbm.1, bf16[256,2304]{1,0:T(8,128)(2,1)} %og_hbm.1, bf16[3,32,4608]{2,1,0:T(8,128)(2,1)} %w_ref.1, f32[36,128]{1,0:T(8,128)} %bitcast.2, s32[3]{0:T(128)} %exp_ref.1, s32[36,128]{1,0:T(8,128)} %bitcast.3), custom_call_target="tpu_custom_call" | custom-call | tf_op jit(solution)/shard_map/pallas_call | solution.py:451
  45.5 0.0 copy-start
  45.5 1.0 %copy-done = bf16[256,2304]{1,0:T(8,128)(2,1)} copy-done((bf16[256,2304]{1,0:T(8,128)(2,1)}, bf16[256,2304]{1,0:T(8,128)(2,1)S(1)}, u32[]{:S(2)}) %copy-start) | copy-done | bytes 1179672
  46.5 0.0 copy-start.1
  46.5 1.0 %copy-done.1 = bf16[3,32,4608]{2,1,0:T(8,128)(2,1)} copy-done((bf16[3,32,4608]{2,1,0:T(8,128)(2,1)}, bf16[3,32,4608]{2,1,0:T(8,128)(2,1)S(1)}, u32[]{:S(2)}) %copy-start.1) | copy-done | bytes 884760
  47.5 2.8 %shard_map.78 = (bf16[256,2304]{1,0:T(8,128)(2,1)}, bf16[3,32,4608]{2,1,0:T(8,128)(2,1)}) custom-call(bf16[256,2304]{1,0:T(8,128)(2,1)} %copy-done, bf16[3,32,4608]{2,1,0:T(8,128)(2,1)} %copy-done.1), custom_call_target="tpu_custom_call" | custom-call | tf_op jit(solution)/shard_map/pallas_call | solution.py:478
Async XLA Ops:
  45.5 1.0 %copy-start = (bf16[256,2304]{1,0:T(8,128)(2,1)}, bf16[256,2304]{1,0:T(8,128)(2,1)S(1)}, u32[]{:S(2)}) copy-start(bf16[256,2304]{1,0:T(8,128)(2,1)S(1)} %get-tuple-element.4.rg_ref) | copy-start | bytes 3538948
  46.5 1.0 %copy-start.1 = (bf16[3,32,4608]{2,1,0:T(8,128)(2,1)}, bf16[3,32,4608]{2,1,0:T(8,128)(2,1)S(1)}, u32[]{:S(2)}) copy-start(bf16[3,32,4608]{2,1,0:T(8,128)(2,1)S(1)} %get-tuple-element.5.wg_ref) | copy-start | bytes 2654212

commit v4 on v3

--- a/solution.py
+++ b/solution.py
@@ -89,6 +89,7 @@
     to_core = (me + 1 - 2 * core, side)
     to_y = (me + 2 - 4 * y, side)
     to_z = [None] + [(zz * 4 + y * 2 + core, side) for zz in z_near[1:]]
+    to_diagonal = [None] + [(target[0], other) for target in to_z[1:]]
     started = []
 
     def send(src, dst, target):
@@ -106,7 +107,7 @@
         return copy
 
     barrier = pltpu.get_barrier_semaphore()
-    partners = [to_x, to_core, to_y] + to_z[1:]
+    partners = [to_x, to_core, to_y] + to_z[1:] + to_diagonal[1:]
     for target in partners:
         pl.semaphore_signal(barrier, inc=1, device_id=target, device_id_type=MESH)
 
@@ -134,7 +135,7 @@
         )
 
     pl.semaphore_wait(barrier, len(partners))
-    w_copies = [send_w(0), send_w(1)]
+    w_copies = [send_w(0)]
     get_res.wait()
     squares = jnp.zeros(column.shape[1:], F32)
     for j in range(blocks):
@@ -143,7 +144,13 @@
     sums = jnp.sum(squares.T, axis=0, keepdims=True)
     sq_mine[...] = jnp.broadcast_to(sums, sq_mine.shape)
     sq_copy = send(sq_mine, sq_peer, to_x)
-    w_copies.append(send_w(2))
+    w_copies += [send_w(1), send_w(2)]
+    shared = []
+
+    def share_w(p):
+        w_copies[p].wait_recv()
+        landed = wbuf.at[other, :, core_rows, pl.ds(cuts[p], cuts[p + 1] - cuts[p])]
+        shared.append(send(landed, landed, to_core))
 
     get_og.wait()
     for j in range(blocks):
@@ -151,6 +158,7 @@
         og_turned[at] = og_ref[:, at].T
     get_w.wait()
     part[side, 2 * rows_w : 3 * rows_w] = dot_nn(wbuf[side, 2], og_turned[...])
+    share_w(0)
     sq_copy.wait_recv()
     total_sq = sq_mine[...] + sq_peer[...]
     inverse = to_column(lax.rsqrt(total_sq / float(2 * cols) + 1e-06))
@@ -161,27 +169,22 @@
         scaled = (unit * gain_ref[pl.ds(first_block + j, 1)]).astype(BF16)
         normed[:, at] = scaled
         normed_turned[at] = scaled.T
+    share_w(1)
     part[side, : 2 * rows_w] = dot_nn(
         wbuf[side, :2].reshape(2 * rows_w, cols), normed_turned[...]
     )
     part_out[side] = part[side].astype(BF16)
     own_part = send(part_out.at[side], part_in.at[side], to_x)
 
-    shared = []
+    share_w(2)
     pair_part = jnp.zeros((2 * rows_w, part.shape[2]), F32)
     down_part = jnp.zeros((rows_w, part.shape[2]), F32)
-    for p in range(pieces + 1):
-        if p < pieces:
-            w_copies[p].wait_recv()
-            landed = wbuf.at[other, :, core_rows, pl.ds(cuts[p], cuts[p + 1] - cuts[p])]
-            shared.append(send(landed, landed, to_core))
-        if p > 0:
-            shared[p - 1].wait_recv()
-            width = cuts[p] - cuts[p - 1]
-            at = slice(cuts[p - 1], cuts[p])
-            weights = wbuf[other, :2, :, at].reshape(2 * rows_w, width)
-            pair_part = pair_part + dot_nn(weights, normed_turned[at])
-            down_part = down_part + dot_nn(wbuf[other, 2, :, at], og_turned[at])
+    for p in range(pieces):
+        shared[p].wait_recv()
+        at = slice(cuts[p], cuts[p + 1])
+        weights = wbuf[other, :2, :, at].reshape(2 * rows_w, cuts[p + 1] - cuts[p])
+        pair_part = pair_part + dot_nn(weights, normed_turned[at])
+        down_part = down_part + dot_nn(wbuf[other, 2, :, at], og_turned[at])
     part[other, : 2 * rows_w] = pair_part
     part[other, 2 * rows_w : 3 * rows_w] = down_part
     part_out[other] = part[other].astype(BF16)
@@ -299,7 +302,12 @@
             turn = sign_ref[pl.ds(first_block + block, 1)] * factor
             for g in range(2):
                 chunk.share[g, i] = (restored[g, i] * turn).astype(BF16)
-        chunk.x_copy = send(chunk.share.at[other], chunk.slots.at[me, side], to_x)
+        landing = chunk.slots.at[me, side]
+        chunk.x_copy = send(chunk.share.at[other], landing, to_x)
+        chunk.z_copies, chunk.diagonals = ([], [])
+        for o in (1, 2, 3):
+            chunk.diagonals.append(send(chunk.share.at[other], landing, to_diagonal[o]))
+            chunk.z_copies.append(send(chunk.share.at[side], landing, to_z[o]))
         chunk.slots[me, side] = chunk.share[side]
 
     def forward(chunk, slot, targets):
@@ -308,7 +316,6 @@
 
     def after_x(chunk):
         chunk.x_copy.wait_recv()
-        chunk.z_copies = forward(chunk, me, to_z[1:])
         to_both = forward(chunk, me, [to_y, to_core])
         chunk.y_copies = to_both[:1]
         chunk.c_copies = to_both[1:]
@@ -316,6 +323,7 @@
     def gather_z(chunk):
         for o in (1, 2, 3):
             chunk.z_copies[o - 1].wait_recv()
+            chunk.diagonals[o - 1].wait_recv()
             to_both = forward(chunk, z_near[o] * 4 + y * 2 + core, [to_y, to_core])
             chunk.y_copies.append(to_both[0])
             chunk.c_copies.append(to_both[1])
@@ -387,18 +395,7 @@
         copy.wait_send()
 
 
-def write_out(rg_ref, wg_ref, rg_out, wg_out, sems):
-    copies = [
-        pltpu.make_async_copy(rg_ref, rg_out, sems.at[0]),
-        pltpu.make_async_copy(wg_ref, wg_out, sems.at[1]),
-    ]
-    for copy in copies:
-        copy.start()
-    for copy in copies:
-        copy.wait()
-
-
-COPIES = 9 + 2 * 21
+COPIES = 9 + 2 * 24
 
 
 def fused(n_dp, residual, out_grad, ffn_weights, norm_gain, exponents, sign_bits):
@@ -448,7 +445,7 @@
         pltpu.SemaphoreType.DMA((COPIES,)),
         pltpu.SemaphoreType.DMA((COPIES,)),
     ]
-    results = pl.pallas_call(
+    return pl.pallas_call(
         functools.partial(kernel, (n_dp, blocks, groups, chunks)),
         out_shape=(
             pltpu.VMEM((tokens, cols), BF16),
@@ -475,13 +472,6 @@
         exponents,
         sign_bits.reshape(-1, 128),
     )
-    return pl.pallas_call(
-        write_out,
-        out_shape=[jax.ShapeDtypeStruct(result.shape, BF16) for result in results],
-        in_specs=[vmem, vmem],
-        out_specs=[hbm, hbm],
-        scratch_shapes=[pltpu.SemaphoreType.DMA((2,))],
-    )(*results)
 
 
 def hadamard():

time: 50.5 us -> 45 us (0.89)
  Pallas kernels: 47.7 us -> 42.3 us
    pallas_call x1 -> x0, Pallas kernels: 2.84 us -> none  [fused(): pl.pallas_call(write_out, out_shape=[jax.ShapeDtypeStruct(result.shape, B...]
    pallas_call x1, Pallas kernels: 44.8 us -> 42.3 us  [fused(): pl.pallas_call(functools.partial(kernel, (n_dp, blocks, groups, chunks)),...]
    unnamed x4 -> x2, local copies, waits for them, and re-layouts: 1.99 us -> 1.93 us
where the time goes in v4:
time: 45 us; the launch traced here: 44.8 us
  Pallas kernels  42.3 us (94%)
  local copies, waits for them, and re-layouts  1.93 us (4%)
  between operations  0.64 us (1%)
    pallas_call x1, Pallas kernels, fused(): pl.pallas_call(functools.partial(kernel, (n_dp, blocks, groups, chunks)),...  42.3 us
    unnamed x2, local copies, waits for them, and re-layouts  1.93 us

profile of v4, /device:TPU:1, one launch (start us, length us, event | category | flops | bytes accessed | tf_op | source)
XLA Modules:
  0.0 44.8 jit_solution(4251959243036550946)
XLA Ops:
  0.6 42.3 %shard_map.77 = (bf16[256,2304]{1,0:T(8,128)(2,1)S(1)}, bf16[3,32,4608]{2,1,0:T(8,128)(2,1)S(1)}) custom-call(bf16[256,2304]{1,0:T(8,128)(2,1)} %res_hbm.1, bf16[256,2304]{1,0:T(8,128)(2,1)} %og_hbm.1, bf16[3,32,4608]{2,1,0:T(8,128)(2,1)} %w_ref.1, f32[36,128]{1,0:T(8,128)} %bitcast.2, s32[3]{0:T(128)} %exp_ref.1, s32[36,128]{1,0:T(8,128)} %bitcast.3), custom_call_target="tpu_custom_call" | custom-call | tf_op jit(solution)/shard_map/pallas_call | solution.py:448
  42.9 1.0 %copy.10 = bf16[256,2304]{1,0:T(8,128)(2,1)} copy(bf16[256,2304]{1,0:T(8,128)(2,1)S(1)} %get-tuple-element.2) | data formatting | bytes 2359296
  43.9 0.9 %copy.11 = bf16[3,32,4608]{2,1,0:T(8,128)(2,1)} copy(bf16[3,32,4608]{2,1,0:T(8,128)(2,1)S(1)} %get-tuple-element.3) | data formatting | bytes 1769472

commit v5 on v4

--- a/solution.py
+++ b/solution.py
@@ -20,7 +20,8 @@
 def split_dot(left, right):
     high = left.astype(BF16)
     low = (left - high.astype(F32)).astype(BF16)
-    return dot_nn(high, right) + dot_nn(low, right)
+    both = dot_nn(jnp.concatenate([high, low], axis=0), right)
+    return both[: left.shape[0]] + both[left.shape[0] :]
 
 
 def signs_256():
@@ -368,34 +369,42 @@
                 og_ref[:, at].astype(F32) + inverse * (feature_grad - unit * row_mean)
             ).astype(BF16)
 
-    one, two = lanes
+    one, two, three = lanes
     all_pairs = blocks // 2
     make_terms(one)
     make_terms(two)
     after_core(one)
+    make_terms(three)
+    after_core(two)
     column[1] = to_column(row_total / float(2 * cols))
     turned = pair_grad.astype(F32).T.astype(BF16)
-    after_core(two)
+    after_y(one)
+    after_core(three)
     make_resid(0, all_pairs // 3)
-    after_y(one)
-    make_resid(all_pairs // 3, 2 * all_pairs // 3)
     after_y(two)
     after_z(one)
+    make_resid(all_pairs // 3, 2 * all_pairs // 3)
+    after_y(three)
+    after_x(one)
     make_resid(2 * all_pairs // 3, all_pairs)
-    after_x(one)
     after_z(two)
     gather_z(one)
     after_x(two)
     gather_y(one)
+    after_z(three)
     gather_z(two)
+    after_x(three)
     gather_y(two)
+    gather_z(three)
     assemble(one)
+    gather_y(three)
     assemble(two)
+    assemble(three)
     for copy in started:
         copy.wait_send()
 
 
-COPIES = 9 + 2 * 24
+COPIES = 9 + 3 * 24
 
 
 def fused(n_dp, residual, out_grad, ffn_weights, norm_gain, exponents, sign_bits):
@@ -404,7 +413,8 @@
     blocks, groups = (cols // 128, bucket // 16)
     all_pairs = blocks // 2
     per_pair = 3 * groups // 2
-    cut = all_pairs // 2
+    half = all_pairs // 2
+    lead_pairs = all_pairs - 2 * half or 1
     vmem = pl.BlockSpec(memory_space=pltpu.VMEM)
     hbm = pl.BlockSpec(memory_space=pltpu.HBM)
     scratch = [
@@ -425,7 +435,11 @@
         pltpu.VMEM((2, 3 * bucket, tokens), BF16),
     ]
     chunks = []
-    for first, pairs in ((0, cut), (cut, all_pairs - cut)):
+    for first, pairs in (
+        (0, lead_pairs),
+        (lead_pairs, half),
+        (lead_pairs + half, all_pairs - lead_pairs - half),
+    ):
         units = pairs * per_pair
         window = -(-units // 4)
         chunks.append((first, pairs, window, [units * zz // 4 for zz in range(4)]))
@@ -565,7 +579,7 @@
 def dispatch(n_dp, n_mp, *args):
     cols = args[0].shape[1]
     bucket = args[2].shape[1]
-    whole = cols % 256 == 0 and bucket % 32 == 0 and cols >= 512
+    whole = cols % 256 == 0 and bucket % 32 == 0 and cols >= 768
     if n_dp == 16 and n_mp == 2 and whole:
         return fused(n_dp, *args)
     return per_device(*args)

time: 45 us -> 46.4 us (1.031)
  Pallas kernels: 42.3 us -> 43.7 us
    pallas_call x1, Pallas kernels: 42.3 us -> 43.7 us  [fused(): pl.pallas_call(functools.partial(kernel, (n_dp, blocks, groups, chunks)),...]
where the time goes in v5:
time: 46.4 us; the launch traced here: 46.3 us
  Pallas kernels  43.7 us (94%)
  local copies, waits for them, and re-layouts  1.93 us (4%)
  between operations  0.64 us (1%)
    pallas_call x1, Pallas kernels, fused(): pl.pallas_call(functools.partial(kernel, (n_dp, blocks, groups, chunks)),...  43.7 us
    unnamed x2, local copies, waits for them, and re-layouts  1.93 us

profile of v5, /device:TPU:1, one launch (start us, length us, event | category | flops | bytes accessed | tf_op | source)
XLA Modules:
  0.0 46.3 jit_solution(11113267025491939834)
XLA Ops:
  0.6 43.7 %shard_map.77 = (bf16[256,2304]{1,0:T(8,128)(2,1)S(1)}, bf16[3,32,4608]{2,1,0:T(8,128)(2,1)S(1)}) custom-call(bf16[256,2304]{1,0:T(8,128)(2,1)} %res_hbm.1, bf16[256,2304]{1,0:T(8,128)(2,1)} %og_hbm.1, bf16[3,32,4608]{2,1,0:T(8,128)(2,1)} %w_ref.1, f32[36,128]{1,0:T(8,128)} %bitcast.2, s32[3]{0:T(128)} %exp_ref.1, s32[36,128]{1,0:T(8,128)} %bitcast.3), custom_call_target="tpu_custom_call" | custom-call | tf_op jit(solution)/shard_map/pallas_call | solution.py:462
  44.3 1.0 %copy.10 = bf16[256,2304]{1,0:T(8,128)(2,1)} copy(bf16[256,2304]{1,0:T(8,128)(2,1)S(1)} %get-tuple-element.2) | data formatting | bytes 2359296
  45.3 0.9 %copy.11 = bf16[3,32,4608]{2,1,0:T(8,128)(2,1)} copy(bf16[3,32,4608]{2,1,0:T(8,128)(2,1)S(1)} %get-tuple-element.3) | data formatting | bytes 1769472

commit v6 on v4

--- a/solution.py
+++ b/solution.py
@@ -404,7 +404,7 @@
     blocks, groups = (cols // 128, bucket // 16)
     all_pairs = blocks // 2
     per_pair = 3 * groups // 2
-    cut = all_pairs // 2
+    cut = all_pairs - all_pairs // 2
     vmem = pl.BlockSpec(memory_space=pltpu.VMEM)
     hbm = pl.BlockSpec(memory_space=pltpu.HBM)
     scratch = [

time: 45 us -> 46.7 us (1.038)
  Pallas kernels: 42.3 us -> 43.9 us
    pallas_call x1, Pallas kernels: 42.3 us -> 43.9 us  [fused(): pl.pallas_call(functools.partial(kernel, (n_dp, blocks, groups, chunks)),...]
where the time goes in v6:
time: 46.7 us; the launch traced here: 46.5 us
  Pallas kernels  43.9 us (94%)
  local copies, waits for them, and re-layouts  1.93 us (4%)
  between operations  0.64 us (1%)
    pallas_call x1, Pallas kernels, fused(): pl.pallas_call(functools.partial(kernel, (n_dp, blocks, groups, chunks)),...  43.9 us
    unnamed x2, local copies, waits for them, and re-layouts  1.93 us

profile of v6, /device:TPU:1, one launch (start us, length us, event | category | flops | bytes accessed | tf_op | source)
XLA Modules:
  0.0 46.5 jit_solution(16753007008760981813)
XLA Ops:
  0.6 43.9 %shard_map.77 = (bf16[256,2304]{1,0:T(8,128)(2,1)S(1)}, bf16[3,32,4608]{2,1,0:T(8,128)(2,1)S(1)}) custom-call(bf16[256,2304]{1,0:T(8,128)(2,1)} %res_hbm.1, bf16[256,2304]{1,0:T(8,128)(2,1)} %og_hbm.1, bf16[3,32,4608]{2,1,0:T(8,128)(2,1)} %w_ref.1, f32[36,128]{1,0:T(8,128)} %bitcast.2, s32[3]{0:T(128)} %exp_ref.1, s32[36,128]{1,0:T(8,128)} %bitcast.3), custom_call_target="tpu_custom_call" | custom-call | tf_op jit(solution)/shard_map/pallas_call | solution.py:448
  44.6 1.0 %copy.10 = bf16[256,2304]{1,0:T(8,128)(2,1)} copy(bf16[256,2304]{1,0:T(8,128)(2,1)S(1)} %get-tuple-element.2) | data formatting | bytes 2359296
  45.6 0.9 %copy.11 = bf16[3,32,4608]{2,1,0:T(8,128)(2,1)} copy(bf16[3,32,4608]{2,1,0:T(8,128)(2,1)S(1)} %get-tuple-element.3) | data formatting | bytes 1769472
